TPU v7x, 256 devices: a whole 4x4x8 slice. The times are simulated.
256 devices in a mesh: pairs: 32 (over y, z), tm: 8 (over x, core).
Axes of the slice: x: 4, y: 4, z: 8, core: 2. Of those that a mesh axis runs over, the one named last changes fastest.
Arguments:
- spectra: bfloat16 [8, 256, 2, 32768], P('tm', 'pairs'), may hold values from -6 to 6
- channel_slot: int32 [256], P('pairs'), may hold values from 0 to 7, as said below
- tile_list: int32 [63, 2], replicated, may hold values from 0 to 31, as said below
- tile_owner: int32 [63], replicated, may hold values from 0 to 31, as said below
Outputs:
- correlations: float32 [128, 64, 256], P('pairs', 'tm')
Inputs may be any that keep to these rules, and one draw needn't show every extreme that they name: `channel_slot`: within each block of 8 channels the values are a permutation of 0..7. `tile_list`: each row (i, j) has j = i or j = i + 1; every such pair of blocks appears exactly once, in some order. `tile_owner`: the owner of the tile in row p of tile_list is that row's i or i + 1; the tile of blocks 0 and 1 is owned by block 1; no owner holds more than 4 tiles, and some owner holds exactly 4.
All inputs are finite; a program needn't handle non-finite values.
Results may differ from a plain program's by a relative error of at most 0.00033.
Values may be sent and summed in bfloat16 or wider, within the bound.
A program may use at most 64 MiB of HBM per device.

v0:
```python
import math
import jax
import jax.numpy as jnp
from jax import lax
from jax.sharding import PartitionSpec as P

LAGS = 256
TILE_CAP = 4


def extended(block, sides, width):
    for axis, dim in sides:
        count = lax.axis_size(axis)
        forward = [(i, i + 1) for i in range(count - 1)]
        backward = [(target, source) for source, target in forward]
        low = lax.ppermute(
            lax.slice_in_dim(block, block.shape[dim] - width, None, axis=dim), axis, forward
        )
        high = lax.ppermute(lax.slice_in_dim(block, 0, width, axis=dim), axis, backward)
        block = jnp.concatenate([low, block, high], axis=dim)
    return block


def lag_table(freq_start, freq_width, bin_count, lag_count):
    freq_ids = freq_start + lax.iota(jnp.int32, freq_width)
    shift_lag = lax.iota(jnp.int32, lag_count) - lag_count // 2
    phase_steps = jnp.mod(freq_ids[:, None] * shift_lag[None, :], 2 * bin_count)
    phase_angle = phase_steps.astype(jnp.float32) * (math.pi / bin_count)
    cosine = jnp.cos(phase_angle).astype(jnp.bfloat16)
    sine_neg = (-jnp.sin(phase_angle)).astype(jnp.bfloat16)
    return jnp.concatenate([cosine, sine_neg], axis=0)


def cross_block(lead_block, tail_block):
    group_count = lead_block.shape[0]
    chan_count = lead_block.shape[1]
    lead_real = lead_block[:, :, 0].astype(jnp.float32)[:, :, None, :]
    lead_imag = lead_block[:, :, 1].astype(jnp.float32)[:, :, None, :]
    tail_real = tail_block[:, :, 0].astype(jnp.float32)[:, None, :, :]
    tail_imag = tail_block[:, :, 1].astype(jnp.float32)[:, None, :, :]
    real_part = lead_real * tail_real + lead_imag * tail_imag
    imag_part = lead_imag * tail_real - lead_real * tail_imag
    joined = jnp.concatenate(
        [real_part.astype(jnp.bfloat16), imag_part.astype(jnp.bfloat16)], axis=-1
    )
    return joined.reshape(group_count, chan_count * chan_count, joined.shape[-1])


def correlate(blocks, lead_pos, tail_pos, norm_scale):
    chan_count = blocks.shape[1]
    bin_count = blocks.shape[3]
    freq_width = min(2048, bin_count)
    slot_count = lead_pos.shape[0]

    def freq_turn(step_index, running):
        freq_start = step_index * freq_width
        freq_piece = lax.dynamic_slice_in_dim(blocks, freq_start, freq_width, 3)
        lead_block = jnp.take(freq_piece, lead_pos, axis=0)
        tail_block = jnp.take(freq_piece, tail_pos, axis=0)
        cross_spec = cross_block(lead_block, tail_block)
        lag_rows = lag_table(freq_start, freq_width, bin_count, LAGS)
        return running + jnp.einsum(
            "spf,fl->spl", cross_spec, lag_rows, preferred_element_type=jnp.float32
        )

    start_sum = jnp.zeros((slot_count, chan_count * chan_count, LAGS), jnp.float32)
    running = lax.fori_loop(0, bin_count // freq_width, freq_turn, start_sum)
    return running * norm_scale


def stack_windows(window_terms):
    summed = lax.psum(window_terms, "tm")
    share_rows = summed.shape[1] // lax.axis_size("tm")
    return lax.dynamic_slice_in_dim(summed, lax.axis_index("tm") * share_rows, share_rows, 1)


def on_device(spectra, channel_slot, tile_list, tile_owner):
    here_index = lax.axis_index("pairs")
    bin_count = spectra.shape[3]
    norm_scale = 1.0 / math.sqrt(2.0 * bin_count * lax.axis_size("tm"))
    ordered = jnp.take(spectra[0], channel_slot, axis=0)
    chan_count = ordered.shape[0]
    tile_count = tile_list.shape[0]
    low_block = tile_list[:, 0]
    high_block = tile_list[:, 1]
    earlier = lax.iota(jnp.int32, tile_count)[:, None] > lax.iota(jnp.int32, tile_count)[None, :]
    slot_rank = jnp.sum((tile_owner[:, None] == tile_owner[None, :]) & earlier, axis=1)
    slot_ids = lax.iota(jnp.int32, TILE_CAP)
    owned_slot = (
        (tile_owner[None, :] == here_index) & (slot_rank[None, :] == slot_ids[:, None])
    ).astype(jnp.int32)
    live_slot = jnp.sum(owned_slot, axis=1)
    slot_low = jnp.sum(owned_slot * low_block[None, :], axis=1)
    slot_high = jnp.sum(owned_slot * high_block[None, :], axis=1)
    widened = extended(ordered, (("pairs", 0),), chan_count)
    blocks = widened.reshape(3, chan_count, widened.shape[1], widened.shape[2])
    lead_pos = jnp.clip(slot_low - here_index + 1, 0, 2)
    tail_pos = jnp.clip(slot_high - here_index + 1, 0, 2)
    window_terms = correlate(blocks, lead_pos, tail_pos, norm_scale)
    window_terms = window_terms * live_slot[:, None, None].astype(jnp.float32)
    return stack_windows(window_terms)


def solution(mesh):
    placed = (P("tm", "pairs", None, None), P("pairs"), P(), P())
    return jax.shard_map(
        on_device, mesh=mesh, in_specs=placed, out_specs=P("pairs", "tm", None), check_vma=False
    )
```

profile of v0, /device:TPU:8, one launch (start us, length us, event | category | flops | bytes accessed | tf_op | source)
XLA Modules:
  0.0 379.8 jit_solution(1595996826397353993)
XLA Ops:
  8.0 2.7 gather_fusion.2
  11.6 7.7 %collective-permute-start.1 = (bf16[8,2,32768]{2,1,0:T(2,128)(2,1)S(1)}, bf16[8,2,32768]{2,1,0:T(2,128)(2,1)S(1)}, u32[]{:S(2)}, u32[]{:S(2)}) collective-permute-start(bf16[8,2,32768]{2,1,0:T(2,128)(2,1)S(1)} %broadcast_select_fusion.2), channel_id=1, source_target_pairs={{8,0},{16,8},{24,16},{32,24},{40,32},{48,40},{56,48},{64,56},{72,6... | collective-permute-start | bytes 3145736 | tf_op jit(solution)/shard_map/ppermute | solution.py:19
  19.3 1.9 collective-permute-start
  21.6 20.1 %collective-permute-done.1 = bf16[8,2,32768]{2,1,0:T(2,128)(2,1)S(1)} collective-permute-done((bf16[8,2,32768]{2,1,0:T(2,128)(2,1)S(1)}, bf16[8,2,32768]{2,1,0:T(2,128)(2,1)S(1)}, u32[]{:S(2)}, u32[]{:S(2)}) %collective-permute-start.1) | collective-permute-done | bytes 1048608 | tf_op jit(solution)/shard_map/ppermute | solution.py:19
  41.7 6.3 %collective-permute-done = bf16[8,2,32768]{2,1,0:T(2,128)(2,1)} collective-permute-done((bf16[8,2,32768]{2,1,0:T(2,128)(2,1)S(1)}, bf16[8,2,32768]{2,1,0:T(2,128)(2,1)}, u32[]{:S(2)}, u32[]{:S(2)}) %collective-permute-start) | collective-permute-done | bytes 1048608 | tf_op jit(solution)/shard_map/ppermute | solution.py:16
  48.0 7.1 %pad_maximum_fusion = bf16[24,2,32768]{2,1,0:T(2,128)(2,1)} fusion(bf16[8,2,32768]{2,1,0:T(2,128)(2,1)S(1)} %collective-permute-done.1, bf16[8,2,32768]{2,1,0:T(2,128)(2,1)S(1)} %broadcast_select_fusion.2, bf16[8,2,32768]{2,1,0:T(2,128)(2,1)} %collective-permute-done), kind=kLoop, calls=%fused_computation.45 | loop fusion | flops 3145728 | bytes 6291456 | tf_op jit(solution)/shard_map/concatenate | solution.py:20
  55.1 254.1 %while.16 = (s32[]{:T(128)}, f32[4,64,256]{2,1,0:T(8,128)S(1)}, bf16[3,8,2,32768]{3,2,1,0:T(2,128)(2,1)}, s32[4]{0:T(128)S(1)}, s32[4]{0:T(128)S(1)}, /*index=5*/s32[]{:T(128)}, s32[]{:T(128)}, s32[]{:T(128)}, s32[]{:T(128)}) while((s32[]{:T(128)}, f32[4,64,256]{2,1,0:T(8,128)S(1)}, bf16[3,8,2,32768]{3,2,1,0:T(2,128)(2,1)}, ...), condition=%wide.region_4.6_spmd.clone, body=%wide.region_3.5_spmd.clone.sunk | while | flops 559026496 | bytes 16148821 | solution.py:67
  56.3 1.1 gather_fusion.1
  57.7 1.1 gather_fusion
  60.7 9.4 %cosine_convert_fusion.2 = (bf16[2048,256]{1,0:T(8,128)(2,1)S(1)}, bf16[2048,256]{1,0:T(8,128)(2,1)S(1)}) fusion(s32[256]{0:T(256)S(1)} %iota_add_fusion.4, s32[2048]{0:T(1024)S(1)} %iota_add_fusion.5), kind=kLoop, calls=%fused_computation.19.clone.1 | loop fusion | flops 8912896 | bytes 2106368 | tf_op jit(solution)/shard_map/while/body/eval_jaxpr/convert_element_type | solution.py:29
  72.2 1.1 gather_fusion.1
  73.5 1.1 gather_fusion
  76.6 9.4 %cosine_convert_fusion.2 = (bf16[2048,256]{1,0:T(8,128)(2,1)S(1)}, bf16[2048,256]{1,0:T(8,128)(2,1)S(1)}) fusion(s32[256]{0:T(256)S(1)} %iota_add_fusion.4, s32[2048]{0:T(1024)S(1)} %iota_add_fusion.5), kind=kLoop, calls=%fused_computation.19.clone.1 | loop fusion | flops 8912896 | bytes 2106368 | tf_op jit(solution)/shard_map/while/body/eval_jaxpr/convert_element_type | solution.py:29
  88.0 1.1 gather_fusion.1
  89.4 1.1 gather_fusion
  92.5 9.4 %cosine_convert_fusion.2 = (bf16[2048,256]{1,0:T(8,128)(2,1)S(1)}, bf16[2048,256]{1,0:T(8,128)(2,1)S(1)}) fusion(s32[256]{0:T(256)S(1)} %iota_add_fusion.4, s32[2048]{0:T(1024)S(1)} %iota_add_fusion.5), kind=kLoop, calls=%fused_computation.19.clone.1 | loop fusion | flops 8912896 | bytes 2106368 | tf_op jit(solution)/shard_map/while/body/eval_jaxpr/convert_element_type | solution.py:29
  103.9 1.1 gather_fusion.1
  105.3 1.1 gather_fusion
  108.4 9.4 %cosine_convert_fusion.2 = (bf16[2048,256]{1,0:T(8,128)(2,1)S(1)}, bf16[2048,256]{1,0:T(8,128)(2,1)S(1)}) fusion(s32[256]{0:T(256)S(1)} %iota_add_fusion.4, s32[2048]{0:T(1024)S(1)} %iota_add_fusion.5), kind=kLoop, calls=%fused_computation.19.clone.1 | loop fusion | flops 8912896 | bytes 2106368 | tf_op jit(solution)/shard_map/while/body/eval_jaxpr/convert_element_type | solution.py:29
  119.8 1.1 gather_fusion.1
  121.2 1.1 gather_fusion
  124.2 9.4 %cosine_convert_fusion.2 = (bf16[2048,256]{1,0:T(8,128)(2,1)S(1)}, bf16[2048,256]{1,0:T(8,128)(2,1)S(1)}) fusion(s32[256]{0:T(256)S(1)} %iota_add_fusion.4, s32[2048]{0:T(1024)S(1)} %iota_add_fusion.5), kind=kLoop, calls=%fused_computation.19.clone.1 | loop fusion | flops 8912896 | bytes 2106368 | tf_op jit(solution)/shard_map/while/body/eval_jaxpr/convert_element_type | solution.py:29
  135.7 1.1 gather_fusion.1
  137.1 1.1 gather_fusion
  140.1 9.4 %cosine_convert_fusion.2 = (bf16[2048,256]{1,0:T(8,128)(2,1)S(1)}, bf16[2048,256]{1,0:T(8,128)(2,1)S(1)}) fusion(s32[256]{0:T(256)S(1)} %iota_add_fusion.4, s32[2048]{0:T(1024)S(1)} %iota_add_fusion.5), kind=kLoop, calls=%fused_computation.19.clone.1 | loop fusion | flops 8912896 | bytes 2106368 | tf_op jit(solution)/shard_map/while/body/eval_jaxpr/convert_element_type | solution.py:29
  151.6 1.1 gather_fusion.1
  152.9 1.1 gather_fusion
  156.0 9.4 %cosine_convert_fusion.2 = (bf16[2048,256]{1,0:T(8,128)(2,1)S(1)}, bf16[2048,256]{1,0:T(8,128)(2,1)S(1)}) fusion(s32[256]{0:T(256)S(1)} %iota_add_fusion.4, s32[2048]{0:T(1024)S(1)} %iota_add_fusion.5), kind=kLoop, calls=%fused_computation.19.clone.1 | loop fusion | flops 8912896 | bytes 2106368 | tf_op jit(solution)/shard_map/while/body/eval_jaxpr/convert_element_type | solution.py:29
  167.4 1.1 gather_fusion.1
  168.8 1.1 gather_fusion
  171.9 9.4 %cosine_convert_fusion.2 = (bf16[2048,256]{1,0:T(8,128)(2,1)S(1)}, bf16[2048,256]{1,0:T(8,128)(2,1)S(1)}) fusion(s32[256]{0:T(256)S(1)} %iota_add_fusion.4, s32[2048]{0:T(1024)S(1)} %iota_add_fusion.5), kind=kLoop, calls=%fused_computation.19.clone.1 | loop fusion | flops 8912896 | bytes 2106368 | tf_op jit(solution)/shard_map/while/body/eval_jaxpr/convert_element_type | solution.py:29
  183.3 1.1 gather_fusion.1
  184.7 1.1 gather_fusion
  187.8 9.4 %cosine_convert_fusion.2 = (bf16[2048,256]{1,0:T(8,128)(2,1)S(1)}, bf16[2048,256]{1,0:T(8,128)(2,1)S(1)}) fusion(s32[256]{0:T(256)S(1)} %iota_add_fusion.4, s32[2048]{0:T(1024)S(1)} %iota_add_fusion.5), kind=kLoop, calls=%fused_computation.19.clone.1 | loop fusion | flops 8912896 | bytes 2106368 | tf_op jit(solution)/shard_map/while/body/eval_jaxpr/convert_element_type | solution.py:29
  199.2 1.1 gather_fusion.1
  200.6 1.1 gather_fusion
  203.7 9.4 %cosine_convert_fusion.2 = (bf16[2048,256]{1,0:T(8,128)(2,1)S(1)}, bf16[2048,256]{1,0:T(8,128)(2,1)S(1)}) fusion(s32[256]{0:T(256)S(1)} %iota_add_fusion.4, s32[2048]{0:T(1024)S(1)} %iota_add_fusion.5), kind=kLoop, calls=%fused_computation.19.clone.1 | loop fusion | flops 8912896 | bytes 2106368 | tf_op jit(solution)/shard_map/while/body/eval_jaxpr/convert_element_type | solution.py:29
  215.1 1.1 gather_fusion.1
  219.5 9.4 %cosine_convert_fusion.2 = (bf16[2048,256]{1,0:T(8,128)(2,1)S(1)}, bf16[2048,256]{1,0:T(8,128)(2,1)S(1)}) fusion(s32[256]{0:T(256)S(1)} %iota_add_fusion.4, s32[2048]{0:T(1024)S(1)} %iota_add_fusion.5), kind=kLoop, calls=%fused_computation.19.clone.1 | loop fusion | flops 8912896 | bytes 2106368 | tf_op jit(solution)/shard_map/while/body/eval_jaxpr/convert_element_type | solution.py:29
  235.4 9.4 %cosine_convert_fusion.2 = (bf16[2048,256]{1,0:T(8,128)(2,1)S(1)}, bf16[2048,256]{1,0:T(8,128)(2,1)S(1)}) fusion(s32[256]{0:T(256)S(1)} %iota_add_fusion.4, s32[2048]{0:T(1024)S(1)} %iota_add_fusion.5), kind=kLoop, calls=%fused_computation.19.clone.1 | loop fusion | flops 8912896 | bytes 2106368 | tf_op jit(solution)/shard_map/while/body/eval_jaxpr/convert_element_type | solution.py:29
  251.3 9.4 %cosine_convert_fusion.2 = (bf16[2048,256]{1,0:T(8,128)(2,1)S(1)}, bf16[2048,256]{1,0:T(8,128)(2,1)S(1)}) fusion(s32[256]{0:T(256)S(1)} %iota_add_fusion.4, s32[2048]{0:T(1024)S(1)} %iota_add_fusion.5), kind=kLoop, calls=%fused_computation.19.clone.1 | loop fusion | flops 8912896 | bytes 2106368 | tf_op jit(solution)/shard_map/while/body/eval_jaxpr/convert_element_type | solution.py:29
  267.2 9.4 %cosine_convert_fusion.2 = (bf16[2048,256]{1,0:T(8,128)(2,1)S(1)}, bf16[2048,256]{1,0:T(8,128)(2,1)S(1)}) fusion(s32[256]{0:T(256)S(1)} %iota_add_fusion.4, s32[2048]{0:T(1024)S(1)} %iota_add_fusion.5), kind=kLoop, calls=%fused_computation.19.clone.1 | loop fusion | flops 8912896 | bytes 2106368 | tf_op jit(solution)/shard_map/while/body/eval_jaxpr/convert_element_type | solution.py:29
  280.0 1.1 gather_fusion
  283.1 9.4 %cosine_convert_fusion.2 = (bf16[2048,256]{1,0:T(8,128)(2,1)S(1)}, bf16[2048,256]{1,0:T(8,128)(2,1)S(1)}) fusion(s32[256]{0:T(256)S(1)} %iota_add_fusion.4, s32[2048]{0:T(1024)S(1)} %iota_add_fusion.5), kind=kLoop, calls=%fused_computation.19.clone.1 | loop fusion | flops 8912896 | bytes 2106368 | tf_op jit(solution)/shard_map/while/body/eval_jaxpr/convert_element_type | solution.py:29
  295.9 1.1 gather_fusion
  299.0 9.4 %cosine_convert_fusion.2 = (bf16[2048,256]{1,0:T(8,128)(2,1)S(1)}, bf16[2048,256]{1,0:T(8,128)(2,1)S(1)}) fusion(s32[256]{0:T(256)S(1)} %iota_add_fusion.4, s32[2048]{0:T(1024)S(1)} %iota_add_fusion.5), kind=kLoop, calls=%fused_computation.19.clone.1 | loop fusion | flops 8912896 | bytes 2106368 | tf_op jit(solution)/shard_map/while/body/eval_jaxpr/convert_element_type | solution.py:29
  310.0 61.6 %all-reduce.2.cloned.1.call-done = f32[4,64,256]{2,1,0:T(8,128)} async-done(((f32[4,64,256]{2,1,0:T(8,128)}), f32[4,64,256]{2,1,0:T(8,128)}) %all-reduce.2.cloned.1.call-update) | async-done | bytes 262160 | tf_op jit(solution)/shard_map/psum | solution.py:72
  371.6 1.4 constant_dynamic-slice_fusion.1
  (301 shorter events, 79.5 us)
Async XLA Ops:
  6.5 1.4 copy-start
  6.5 365.1 %all-reduce.2.cloned.1.call-start = ((), (), s32[]{:S(2)}) async-start(), calls=%async_computation | async-start | bytes 524288 | tf_op jit(solution)/shard_map/psum | solution.py:72
  8.0 13.3 %copy-start.2 = (s32[63]{0:T(128)S(1)}, s32[63]{0:T(128)}, u32[]{:S(2)}) copy-start(s32[63]{0:T(128)} %param.11) | copy-start | bytes 760
  8.0 13.5 %copy-start.1 = (s32[63,2]{0,1:T(2,128)S(1)}, s32[63,2]{0,1:T(2,128)}, u32[]{:S(2)}) copy-start(s32[63,2]{0,1:T(2,128)} %param.10) | copy-start | bytes 1516
  11.6 30.1 %collective-permute-start.1 = (bf16[8,2,32768]{2,1,0:T(2,128)(2,1)S(1)}, bf16[8,2,32768]{2,1,0:T(2,128)(2,1)S(1)}, u32[]{:S(2)}, u32[]{:S(2)}) collective-permute-start(bf16[8,2,32768]{2,1,0:T(2,128)(2,1)S(1)} %broadcast_select_fusion.2), channel_id=1, source_target_pairs={{8,0},{16,8},{24,16},{32,24},{40,32},{48,40},{56,48},{64,56},{72,6... | collective-permute-start | bytes 3145736 | tf_op jit(solution)/shard_map/ppermute | solution.py:19
  19.3 28.7 %collective-permute-start = (bf16[8,2,32768]{2,1,0:T(2,128)(2,1)S(1)}, bf16[8,2,32768]{2,1,0:T(2,128)(2,1)}, u32[]{:S(2)}, u32[]{:S(2)}) collective-permute-start(bf16[8,2,32768]{2,1,0:T(2,128)(2,1)S(1)} %broadcast_select_fusion.2), channel_id=1, source_target_pairs={{0,8},{8,16},{16,24},{24,32},{32,40},{40,48},{48,56},{56,64},{64,7... | collective-permute-start | bytes 3145736 | tf_op jit(solution)/shard_map/ppermute | solution.py:16
Sparse Core Ops, SparseCore 0:
  310.1 61.4 all-reduce.1
where the time goes:
time: 381 us; the launch traced here: 380 us
  other arithmetic  192 us (50%)
  waiting for transfers between devices  88 us (23%)
  local copies, waits for them, and re-layouts  60.9 us (16%)
  between operations  13.5 us (4%)
  matrix products  12.9 us (3%)
  starting transfers between devices  9.57 us (3%)
    convert_element_type x16, other arithmetic, lag_table(): cosine = jnp.cos(phase_angle).astype(jnp.bfloat16)  151 us
    psum x1, waiting for transfers between devices, stack_windows(): summed = lax.psum(window_terms, 'tm')  61.6 us
    ppermute x1, waiting for transfers between devices, extended(): lax.ppermute(lax.slice_in_dim(block, 0, width, axis=dim), axis, backward)  20.1 us
    gather x16, local copies, waits for them, and re-layouts, freq_turn(): tail_block = jnp.take(freq_piece, tail_pos, axis=0)  17.2 us
    gather x16, local copies, waits for them, and re-layouts, freq_turn(): lead_block = jnp.take(freq_piece, lead_pos, axis=0)  17.2 us
    dynamic_slice x16, local copies, waits for them, and re-layouts, freq_turn(): freq_piece = lax.dynamic_slice_in_dim(blocks, freq_start, freq_width, 3)  17.1 us
    dot_general x16, matrix products, freq_turn(): jnp.einsum('spf,fl->spl', cross_spec, lag_rows, preferred_element_type=jn...  12.9 us
    convert_element_type x16, other arithmetic, cross_block(): real_part.astype(jnp.bfloat16)  8.57 us
  transfers between devices with their start and end apart: 3, of which 3 were waited for; matrix products, arithmetic and copies ran while one was open for 0% of the time, Pallas kernels for 0%

commit v1 on v0

--- a/solution.py
+++ b/solution.py
@@ -69,7 +69,9 @@
 
 
 def stack_windows(window_terms):
-    summed = lax.psum(window_terms, "tm")
+    summed = window_terms
+    for hop in (1, 2, 4):
+        summed = summed + lax.ppermute(summed, "tm", [(dev, dev ^ hop) for dev in range(8)])
     share_rows = summed.shape[1] // lax.axis_size("tm")
     return lax.dynamic_slice_in_dim(summed, lax.axis_index("tm") * share_rows, share_rows, 1)
 

time: 381 us -> 324 us (0.85)
  waiting for transfers between devices: 88 us -> 40.6 us
  between operations: 13.5 us -> 0.13 us
  starting transfers between devices: 9.57 us -> 14.5 us
    psum x1 -> x0, waiting for transfers between devices: 61.6 us -> none  [stack_windows(): summed = lax.psum(window_terms, 'tm')]
    ppermute x0 -> x3, waiting for transfers between devices: none -> 14.2 us  [stack_windows(): lax.ppermute(summed, 'tm', [(dev, dev ^ hop) for dev in range(8)])]
    ppermute x0 -> x3, starting transfers between devices: none -> 4.92 us  [stack_windows(): lax.ppermute(summed, 'tm', [(dev, dev ^ hop) for dev in range(8)])]
  transfers between devices with their start and end apart: 3 -> 5, of which waited for: 3 -> 5; matrix products, arithmetic and copies ran while one was open for 0% -> 0% of each run, Pallas kernels for 0% -> 0%
where the time goes in v1:
time: 324 us; the launch traced here: 323 us
  other arithmetic  193 us (60%)
  local copies, waits for them, and re-layouts  59.6 us (18%)
  waiting for transfers between devices  40.6 us (13%)
  starting transfers between devices  14.5 us (4%)
  matrix products  12.9 us (4%)
    convert_element_type x16, other arithmetic, lag_table(): cosine = jnp.cos(phase_angle).astype(jnp.bfloat16)  151 us
    ppermute x1, waiting for transfers between devices, extended(): lax.ppermute(lax.slice_in_dim(block, 0, width, axis=dim), axis, backward)  20.1 us
    gather x16, local copies, waits for them, and re-layouts, freq_turn(): lead_block = jnp.take(freq_piece, lead_pos, axis=0)  17.2 us
    gather x16, local copies, waits for them, and re-layouts, freq_turn(): tail_block = jnp.take(freq_piece, tail_pos, axis=0)  17.2 us
    dynamic_slice x16, local copies, waits for them, and re-layouts, freq_turn(): freq_piece = lax.dynamic_slice_in_dim(blocks, freq_start, freq_width, 3)  17.1 us
    ppermute x3, waiting for transfers between devices, stack_windows(): lax.ppermute(summed, 'tm', [(dev, dev ^ hop) for dev in range(8)])  14.2 us
    dot_general x16, matrix products, freq_turn(): jnp.einsum('spf,fl->spl', cross_spec, lag_rows, preferred_element_type=jn...  12.9 us
    convert_element_type x16, other arithmetic, cross_block(): real_part.astype(jnp.bfloat16)  8.99 us
  transfers between devices with their start and end apart: 5, of which 5 were waited for; matrix products, arithmetic and copies ran while one was open for 0% of the time, Pallas kernels for 0%

profile of v1, /device:TPU:8, one launch (start us, length us, event | category | flops | bytes accessed | tf_op | source)
XLA Modules:
  0.0 323.4 jit_solution(16982035964474105984)
XLA Ops:
  1.4 2.7 gather_fusion.2
  5.1 7.7 %collective-permute-start.1 = (bf16[8,2,32768]{2,1,0:T(2,128)(2,1)S(1)}, bf16[8,2,32768]{2,1,0:T(2,128)(2,1)}, u32[]{:S(2)}, u32[]{:S(2)}) collective-permute-start(bf16[8,2,32768]{2,1,0:T(2,128)(2,1)S(1)} %broadcast_select_fusion.2), channel_id=1, source_target_pairs={{8,0},{16,8},{24,16},{32,24},{40,32},{48,40},{56,48},{64,56},{72,6... | collective-permute-start | bytes 3145736 | tf_op jit(solution)/shard_map/ppermute | solution.py:19
  12.7 1.9 collective-permute-start
  15.1 20.1 %collective-permute-done.1 = bf16[8,2,32768]{2,1,0:T(2,128)(2,1)} collective-permute-done((bf16[8,2,32768]{2,1,0:T(2,128)(2,1)S(1)}, bf16[8,2,32768]{2,1,0:T(2,128)(2,1)}, u32[]{:S(2)}, u32[]{:S(2)}) %collective-permute-start.1) | collective-permute-done | bytes 1048608 | tf_op jit(solution)/shard_map/ppermute | solution.py:19
  35.1 6.3 %collective-permute-done = bf16[8,2,32768]{2,1,0:T(2,128)(2,1)} collective-permute-done((bf16[8,2,32768]{2,1,0:T(2,128)(2,1)S(1)}, bf16[8,2,32768]{2,1,0:T(2,128)(2,1)}, u32[]{:S(2)}, u32[]{:S(2)}) %collective-permute-start) | collective-permute-done | bytes 1048608 | tf_op jit(solution)/shard_map/ppermute | solution.py:16
  41.5 7.4 %pad_maximum_fusion = bf16[24,2,32768]{2,1,0:T(2,128)(2,1)} fusion(bf16[8,2,32768]{2,1,0:T(2,128)(2,1)} %collective-permute-done.1, bf16[8,2,32768]{2,1,0:T(2,128)(2,1)S(1)} %broadcast_select_fusion.2, bf16[8,2,32768]{2,1,0:T(2,128)(2,1)} %collective-permute-done), kind=kLoop, calls=%fused_computation.45 | loop fusion | flops 3145728 | bytes 6291456 | tf_op jit(solution)/shard_map/concatenate | solution.py:20
  48.9 254.5 %while.16 = (s32[]{:T(128)}, f32[4,64,256]{2,1,0:T(8,128)S(1)}, bf16[3,8,2,32768]{3,2,1,0:T(2,128)(2,1)}, s32[4]{0:T(128)S(1)}, s32[4]{0:T(128)S(1)}, /*index=5*/s32[]{:T(128)}, s32[]{:T(128)}, s32[]{:T(128)}, s32[]{:T(128)}) while((s32[]{:T(128)}, f32[4,64,256]{2,1,0:T(8,128)S(1)}, bf16[3,8,2,32768]{3,2,1,0:T(2,128)(2,1)}, ...), condition=%wide.region_4.6_spmd.clone, body=%wide.region_3.5_spmd.clone.sunk | while | flops 559026496 | bytes 16148821 | solution.py:67
  50.0 1.1 gather_fusion.1
  51.4 1.1 gather_fusion
  54.5 9.4 %cosine_convert_fusion.2 = (bf16[2048,256]{1,0:T(8,128)(2,1)S(1)}, bf16[2048,256]{1,0:T(8,128)(2,1)S(1)}) fusion(s32[256]{0:T(256)S(1)} %iota_add_fusion.4, s32[2048]{0:T(1024)S(1)} %iota_add_fusion.5), kind=kLoop, calls=%fused_computation.19.clone.1 | loop fusion | flops 8912896 | bytes 2106368 | tf_op jit(solution)/shard_map/while/body/eval_jaxpr/convert_element_type | solution.py:29
  65.9 1.1 gather_fusion.1
  67.3 1.1 gather_fusion
  70.4 9.4 %cosine_convert_fusion.2 = (bf16[2048,256]{1,0:T(8,128)(2,1)S(1)}, bf16[2048,256]{1,0:T(8,128)(2,1)S(1)}) fusion(s32[256]{0:T(256)S(1)} %iota_add_fusion.4, s32[2048]{0:T(1024)S(1)} %iota_add_fusion.5), kind=kLoop, calls=%fused_computation.19.clone.1 | loop fusion | flops 8912896 | bytes 2106368 | tf_op jit(solution)/shard_map/while/body/eval_jaxpr/convert_element_type | solution.py:29
  81.8 1.1 gather_fusion.1
  83.2 1.1 gather_fusion
  86.3 9.4 %cosine_convert_fusion.2 = (bf16[2048,256]{1,0:T(8,128)(2,1)S(1)}, bf16[2048,256]{1,0:T(8,128)(2,1)S(1)}) fusion(s32[256]{0:T(256)S(1)} %iota_add_fusion.4, s32[2048]{0:T(1024)S(1)} %iota_add_fusion.5), kind=kLoop, calls=%fused_computation.19.clone.1 | loop fusion | flops 8912896 | bytes 2106368 | tf_op jit(solution)/shard_map/while/body/eval_jaxpr/convert_element_type | solution.py:29
  97.8 1.1 gather_fusion.1
  99.1 1.1 gather_fusion
  102.2 9.4 %cosine_convert_fusion.2 = (bf16[2048,256]{1,0:T(8,128)(2,1)S(1)}, bf16[2048,256]{1,0:T(8,128)(2,1)S(1)}) fusion(s32[256]{0:T(256)S(1)} %iota_add_fusion.4, s32[2048]{0:T(1024)S(1)} %iota_add_fusion.5), kind=kLoop, calls=%fused_computation.19.clone.1 | loop fusion | flops 8912896 | bytes 2106368 | tf_op jit(solution)/shard_map/while/body/eval_jaxpr/convert_element_type | solution.py:29
  113.7 1.1 gather_fusion.1
  115.0 1.1 gather_fusion
  118.1 9.4 %cosine_convert_fusion.2 = (bf16[2048,256]{1,0:T(8,128)(2,1)S(1)}, bf16[2048,256]{1,0:T(8,128)(2,1)S(1)}) fusion(s32[256]{0:T(256)S(1)} %iota_add_fusion.4, s32[2048]{0:T(1024)S(1)} %iota_add_fusion.5), kind=kLoop, calls=%fused_computation.19.clone.1 | loop fusion | flops 8912896 | bytes 2106368 | tf_op jit(solution)/shard_map/while/body/eval_jaxpr/convert_element_type | solution.py:29
  129.6 1.1 gather_fusion.1
  131.0 1.1 gather_fusion
  134.0 9.4 %cosine_convert_fusion.2 = (bf16[2048,256]{1,0:T(8,128)(2,1)S(1)}, bf16[2048,256]{1,0:T(8,128)(2,1)S(1)}) fusion(s32[256]{0:T(256)S(1)} %iota_add_fusion.4, s32[2048]{0:T(1024)S(1)} %iota_add_fusion.5), kind=kLoop, calls=%fused_computation.19.clone.1 | loop fusion | flops 8912896 | bytes 2106368 | tf_op jit(solution)/shard_map/while/body/eval_jaxpr/convert_element_type | solution.py:29
  145.5 1.1 gather_fusion.1
  146.9 1.1 gather_fusion
  150.0 9.4 %cosine_convert_fusion.2 = (bf16[2048,256]{1,0:T(8,128)(2,1)S(1)}, bf16[2048,256]{1,0:T(8,128)(2,1)S(1)}) fusion(s32[256]{0:T(256)S(1)} %iota_add_fusion.4, s32[2048]{0:T(1024)S(1)} %iota_add_fusion.5), kind=kLoop, calls=%fused_computation.19.clone.1 | loop fusion | flops 8912896 | bytes 2106368 | tf_op jit(solution)/shard_map/while/body/eval_jaxpr/convert_element_type | solution.py:29
  161.4 1.1 gather_fusion.1
  162.8 1.1 gather_fusion
  165.9 9.4 %cosine_convert_fusion.2 = (bf16[2048,256]{1,0:T(8,128)(2,1)S(1)}, bf16[2048,256]{1,0:T(8,128)(2,1)S(1)}) fusion(s32[256]{0:T(256)S(1)} %iota_add_fusion.4, s32[2048]{0:T(1024)S(1)} %iota_add_fusion.5), kind=kLoop, calls=%fused_computation.19.clone.1 | loop fusion | flops 8912896 | bytes 2106368 | tf_op jit(solution)/shard_map/while/body/eval_jaxpr/convert_element_type | solution.py:29
  177.3 1.1 gather_fusion.1
  178.7 1.1 gather_fusion
  181.8 9.4 %cosine_convert_fusion.2 = (bf16[2048,256]{1,0:T(8,128)(2,1)S(1)}, bf16[2048,256]{1,0:T(8,128)(2,1)S(1)}) fusion(s32[256]{0:T(256)S(1)} %iota_add_fusion.4, s32[2048]{0:T(1024)S(1)} %iota_add_fusion.5), kind=kLoop, calls=%fused_computation.19.clone.1 | loop fusion | flops 8912896 | bytes 2106368 | tf_op jit(solution)/shard_map/while/body/eval_jaxpr/convert_element_type | solution.py:29
  197.7 9.4 %cosine_convert_fusion.2 = (bf16[2048,256]{1,0:T(8,128)(2,1)S(1)}, bf16[2048,256]{1,0:T(8,128)(2,1)S(1)}) fusion(s32[256]{0:T(256)S(1)} %iota_add_fusion.4, s32[2048]{0:T(1024)S(1)} %iota_add_fusion.5), kind=kLoop, calls=%fused_computation.19.clone.1 | loop fusion | flops 8912896 | bytes 2106368 | tf_op jit(solution)/shard_map/while/body/eval_jaxpr/convert_element_type | solution.py:29
  209.1 1.1 gather_fusion.1
  213.6 9.4 %cosine_convert_fusion.2 = (bf16[2048,256]{1,0:T(8,128)(2,1)S(1)}, bf16[2048,256]{1,0:T(8,128)(2,1)S(1)}) fusion(s32[256]{0:T(256)S(1)} %iota_add_fusion.4, s32[2048]{0:T(1024)S(1)} %iota_add_fusion.5), kind=kLoop, calls=%fused_computation.19.clone.1 | loop fusion | flops 8912896 | bytes 2106368 | tf_op jit(solution)/shard_map/while/body/eval_jaxpr/convert_element_type | solution.py:29
  226.4 1.1 gather_fusion
  229.5 9.4 %cosine_convert_fusion.2 = (bf16[2048,256]{1,0:T(8,128)(2,1)S(1)}, bf16[2048,256]{1,0:T(8,128)(2,1)S(1)}) fusion(s32[256]{0:T(256)S(1)} %iota_add_fusion.4, s32[2048]{0:T(1024)S(1)} %iota_add_fusion.5), kind=kLoop, calls=%fused_computation.19.clone.1 | loop fusion | flops 8912896 | bytes 2106368 | tf_op jit(solution)/shard_map/while/body/eval_jaxpr/convert_element_type | solution.py:29
  245.4 9.4 %cosine_convert_fusion.2 = (bf16[2048,256]{1,0:T(8,128)(2,1)S(1)}, bf16[2048,256]{1,0:T(8,128)(2,1)S(1)}) fusion(s32[256]{0:T(256)S(1)} %iota_add_fusion.4, s32[2048]{0:T(1024)S(1)} %iota_add_fusion.5), kind=kLoop, calls=%fused_computation.19.clone.1 | loop fusion | flops 8912896 | bytes 2106368 | tf_op jit(solution)/shard_map/while/body/eval_jaxpr/convert_element_type | solution.py:29
  261.3 9.4 %cosine_convert_fusion.2 = (bf16[2048,256]{1,0:T(8,128)(2,1)S(1)}, bf16[2048,256]{1,0:T(8,128)(2,1)S(1)}) fusion(s32[256]{0:T(256)S(1)} %iota_add_fusion.4, s32[2048]{0:T(1024)S(1)} %iota_add_fusion.5), kind=kLoop, calls=%fused_computation.19.clone.1 | loop fusion | flops 8912896 | bytes 2106368 | tf_op jit(solution)/shard_map/while/body/eval_jaxpr/convert_element_type | solution.py:29
  277.2 9.4 %cosine_convert_fusion.2 = (bf16[2048,256]{1,0:T(8,128)(2,1)S(1)}, bf16[2048,256]{1,0:T(8,128)(2,1)S(1)}) fusion(s32[256]{0:T(256)S(1)} %iota_add_fusion.4, s32[2048]{0:T(1024)S(1)} %iota_add_fusion.5), kind=kLoop, calls=%fused_computation.19.clone.1 | loop fusion | flops 8912896 | bytes 2106368 | tf_op jit(solution)/shard_map/while/body/eval_jaxpr/convert_element_type | solution.py:29
  293.1 9.4 %cosine_convert_fusion.2 = (bf16[2048,256]{1,0:T(8,128)(2,1)S(1)}, bf16[2048,256]{1,0:T(8,128)(2,1)S(1)}) fusion(s32[256]{0:T(256)S(1)} %iota_add_fusion.4, s32[2048]{0:T(1024)S(1)} %iota_add_fusion.5), kind=kLoop, calls=%fused_computation.19.clone.1 | loop fusion | flops 8912896 | bytes 2106368 | tf_op jit(solution)/shard_map/while/body/eval_jaxpr/convert_element_type | solution.py:29
  303.6 1.5 collective-permute-done.2
  305.2 1.6 collective-permute-start.3
  306.8 6.8 %collective-permute-done.3 = f32[4,64,256]{2,1,0:T(8,128)S(1)} collective-permute-done((f32[4,64,256]{2,1,0:T(8,128)S(1)}, f32[4,64,256]{2,1,0:T(8,128)S(1)}, u32[]{:S(2)}, u32[]{:S(2)}) %collective-permute-start.3) | collective-permute-done | bytes 262176 | tf_op jit(solution)/shard_map/ppermute | solution.py:74
  313.7 3.2 collective-permute-start.4
  316.9 5.9 %collective-permute-done.4 = f32[4,64,256]{2,1,0:T(8,128)S(1)} collective-permute-done((f32[4,64,256]{2,1,0:T(8,128)S(1)}, f32[4,64,256]{2,1,0:T(8,128)S(1)}, u32[]{:S(2)}, u32[]{:S(2)}) %collective-permute-start.4) | collective-permute-done | bytes 262176 | tf_op jit(solution)/shard_map/ppermute | solution.py:74
  (306 shorter events, 83.3 us)
Async XLA Ops:
  0.0 1.4 copy-start
  1.4 13.3 %copy-start.2 = (s32[63]{0:T(128)S(1)}, s32[63]{0:T(128)}, u32[]{:S(2)}) copy-start(s32[63]{0:T(128)} %param.11) | copy-start | bytes 760
  1.4 13.5 %copy-start.1 = (s32[63,2]{0,1:T(2,128)S(1)}, s32[63,2]{0,1:T(2,128)}, u32[]{:S(2)}) copy-start(s32[63,2]{0,1:T(2,128)} %param.10) | copy-start | bytes 1516
  5.1 30.1 %collective-permute-start.1 = (bf16[8,2,32768]{2,1,0:T(2,128)(2,1)S(1)}, bf16[8,2,32768]{2,1,0:T(2,128)(2,1)}, u32[]{:S(2)}, u32[]{:S(2)}) collective-permute-start(bf16[8,2,32768]{2,1,0:T(2,128)(2,1)S(1)} %broadcast_select_fusion.2), channel_id=1, source_target_pairs={{8,0},{16,8},{24,16},{32,24},{40,32},{48,40},{56,48},{64,56},{72,6... | collective-permute-start | bytes 3145736 | tf_op jit(solution)/shard_map/ppermute | solution.py:19
  12.7 28.7 %collective-permute-start = (bf16[8,2,32768]{2,1,0:T(2,128)(2,1)S(1)}, bf16[8,2,32768]{2,1,0:T(2,128)(2,1)}, u32[]{:S(2)}, u32[]{:S(2)}) collective-permute-start(bf16[8,2,32768]{2,1,0:T(2,128)(2,1)S(1)} %broadcast_select_fusion.2), channel_id=1, source_target_pairs={{0,8},{8,16},{16,24},{24,32},{32,40},{40,48},{48,56},{56,64},{64,7... | collective-permute-start | bytes 3145736 | tf_op jit(solution)/shard_map/ppermute | solution.py:16
  303.5 1.6 collective-permute-start.2
  305.2 8.4 %collective-permute-start.3 = (f32[4,64,256]{2,1,0:T(8,128)S(1)}, f32[4,64,256]{2,1,0:T(8,128)S(1)}, u32[]{:S(2)}, u32[]{:S(2)}) collective-permute-start(f32[4,64,256]{2,1,0:T(8,128)S(1)} %fusion.17), channel_id=1, source_target_pairs={{0,2},{1,3},{2,0},{3,1},{4,6},{5,7},{6,4},{7,5},{8,10},{9,11},{10,... | collective-permute-start | bytes 786440 | tf_op jit(solution)/shard_map/ppermute | solution.py:74
  313.7 9.1 %collective-permute-start.4 = (f32[4,64,256]{2,1,0:T(8,128)S(1)}, f32[4,64,256]{2,1,0:T(8,128)S(1)}, u32[]{:S(2)}, u32[]{:S(2)}) collective-permute-start(f32[4,64,256]{2,1,0:T(8,128)S(1)} %add.123), channel_id=1, source_target_pairs={{0,4},{1,5},{2,6},{3,7},{4,0},{5,1},{6,2},{7,3},{8,12},{9,13},{10,... | collective-permute-start | bytes 786440 | tf_op jit(solution)/shard_map/ppermute | solution.py:74
